TPU v7x, 32 devices: a whole 2x2x4 slice. The times are simulated.
32 devices in a mesh: stream: 4 (over y, core), cross: 8 (over z, x).
Axes of the slice: x: 2, y: 2, z: 4, core: 2. Of those that a mesh axis runs over, the one named last changes fastest.
Arguments:
- pressure: float32 [96, 64, 128], P('stream', 'cross'), may hold values from -6 to 6
- geo_diag: float32 [3, 96, 64, 128], P(None, 'stream', 'cross'), may hold values from 0.004 to 0.04
- geo_off: float32 [3, 96, 64, 128], P(None, 'stream', 'cross'), may hold values from -0.008 to 0.008
- modes_first: float32 [12, 10, 10], P('stream'), may hold values from -2 to 2
- modes_second: float32 [8, 10, 10], P('cross'), may hold values from -2 to 2
- modes_third: float32 [16, 10, 10], replicated, may hold values from -2 to 2
- eigen_first: float32 [12, 10], P('stream'), may hold values from 0.3 to 3
- eigen_second: float32 [8, 10], P('cross'), may hold values from 0.3 to 3
- eigen_third: float32 [16, 10], replicated, may hold values from 0.3 to 3
Outputs:
- operator_out: float32 [96, 64, 128], P('stream', 'cross')
- preconditioned: float32 [96, 64, 128], P('stream', 'cross')
All inputs are finite; a program needn't handle non-finite values.
Results may differ from a plain program's by a relative error of at most 0.00013.
Values sent between devices are 32-bit elements; how exact they have to be, the bound alone decides.
No kernel may reach another device: no remote copies, remote signals or barrier semaphores. Data moves between devices by JAX's collectives and lax.ppermute only.
A program may use at most 64 MiB of HBM per device.

v0:
```python
import functools

import jax
import jax.numpy as jnp
import numpy as np
from jax import lax
from jax.experimental import pallas as pl
from jax.experimental.pallas import tpu as pltpu
from jax.sharding import PartitionSpec as P

N1 = 8
F32 = jnp.float32
BF16 = jnp.bfloat16
HIGHEST = lax.Precision.HIGHEST
VMEM_LIMIT = 16 * 2**20
VMEM = pl.BlockSpec(memory_space=pltpu.VMEM)


def legendre_values(nodes, degree):
    table = np.zeros((nodes.shape[0], degree + 1))
    table[:, 0] = 1.0
    table[:, 1] = nodes
    for order in range(2, degree + 1):
        table[:, order] = (
            (2 * order - 1) * nodes * table[:, order - 1] - (order - 1) * table[:, order - 2]
        ) / order
    return table


def derivative_table(points):
    degree = points - 1
    nodes = np.cos(np.pi * np.arange(points) / degree)
    for sweep in range(100):
        table = legendre_values(nodes, degree)
        nodes = nodes - (nodes * table[:, degree] - table[:, degree - 1]) / (
            points * table[:, degree]
        )
    gll_nodes = nodes[::-1]
    legendre_at = legendre_values(gll_nodes, degree)[:, degree]
    diff_table = np.zeros((points, points))
    for first_index in range(points):
        for second_index in range(points):
            if first_index != second_index:
                diff_table[first_index, second_index] = legendre_at[first_index] / (
                    legendre_at[second_index] * (gll_nodes[first_index] - gll_nodes[second_index])
                )
    diff_table[0, 0] = -degree * (degree + 1) / 4.0
    diff_table[degree, degree] = degree * (degree + 1) / 4.0
    return diff_table


def round_up(count, unit):
    return -(-count // unit) * unit


def dot(left, right, dims=((1,), (0,)), precision=None):
    return lax.dot_general(
        left, right, (dims, ((), ())), precision=precision, preferred_element_type=F32
    )


def split(value):
    high = value.astype(BF16)
    return high, (value - high.astype(F32)).astype(BF16)


def split3(value):
    high = value.astype(BF16)
    rest = value - high.astype(F32)
    mid = rest.astype(BF16)
    return high, mid, (rest - mid.astype(F32)).astype(BF16)


def stacked(value):
    high, low = split(value)
    return jnp.concatenate([high, low, high], 0)


def abreast(value):
    high, low = split(value)
    return jnp.concatenate([high, high, low], 1)


def even(index):
    return lax.rem(index, 2) == 0


def diff_parts():
    table = derivative_table(N1).astype(np.float32)
    high = table.astype(jnp.bfloat16).astype(np.float32)
    low = (table - high).astype(jnp.bfloat16).astype(np.float32)
    row, column = ramps(N1, N1)
    place = row * N1 + column
    found = []
    for part in (high, low):
        value = jnp.zeros((N1, N1), F32)
        for k, entry in enumerate(part.reshape(-1)):
            if entry:
                value = jnp.where(place == k, float(entry), value)
        found.append(value.astype(BF16))
    return found


def operator_factors(blocks):
    def kron(part, count, inner, turned):
        row, column = ramps(count, N1)
        quotient, rest = over(row, N1)
        pick = mask((rest if inner else quotient) == column)
        value = dot(pick, part, ((1,), (1 if turned else 0,))).astype(BF16)
        row, column = ramps(N1, count)
        value = dot(value, mask(over(column, N1)[1 if inner else 0] == row))
        row, column = ramps(count, count)
        row, column = over(row, N1), over(column, N1)
        same = row[0] == column[0] if inner else row[1] == column[1]
        return jnp.where(same, value, 0.0).astype(BF16)

    parts = diff_parts()
    box = N1 * N1
    high, low = [
        jnp.concatenate([kron(part, box, False, False), kron(part, box, True, False)], 0) for part in parts
    ]
    grad = jnp.concatenate([high, high, low], 1)
    high, low = [
        jnp.concatenate([kron(part, box, False, True), kron(part, box, True, True)], 1) for part in parts
    ]
    back = jnp.concatenate([high, high, low], 1)
    high, low = [kron(part, blocks * N1, True, True) for part in parts]
    third = jnp.concatenate([high, low, high], 0)
    high, low = [kron(part, blocks * N1, True, False) for part in parts]
    return grad, third, back, jnp.concatenate([high, low, high], 0)


def local_kernel(*refs):
    count = 6
    sources, outs, scratch = refs[:count], refs[count : count + 6], refs[count + 6 :]
    lp_ref, near_ref, far_ref, mf_ref, ef_ref, es_ref = outs
    p_ref, gd_ref, go_ref, sems = scratch
    targets = (p_ref, gd_ref, go_ref, mf_ref, ef_ref, es_ref)
    copies = [
        pltpu.make_async_copy(source, target, sems.at[k])
        for k, (source, target) in enumerate(zip(sources, targets))
    ]
    for copy in copies:
        copy.start()
    layers, rows, width = p_ref.shape
    grad, third_grad, back, third_back = operator_factors(width // N1)
    copies[0].wait()
    first_blocks = layers // N1
    box = N1 * rows
    modes = mf_ref.shape[0]
    p_all = p_ref[...].reshape(layers * rows, width)
    third = dot(abreast(p_all), third_grad)
    grads = [
        dot(grad, stacked(p_all[a * box : (a + 1) * box])) for a in range(first_blocks)
    ]
    for k in (1, 2):
        copies[k].wait()
    for a in range(first_blocks):
        here = slice(a * box, (a + 1) * box)
        one, two, three = grads[a][:box], grads[a][box:], third[here]
        g = [
            gd_ref[k, a * N1 : (a + 1) * N1].reshape(box, width) for k in range(3)
        ] + [go_ref[k, a * N1 : (a + 1) * N1].reshape(box, width) for k in range(3)]
        flux_one = g[0] * one + g[3] * two + g[4] * three
        flux_two = g[3] * one + g[1] * two + g[5] * three
        flux_three = g[4] * one + g[5] * two + g[2] * three
        lp_ref[here, :] = dot(
            back, stacked(jnp.concatenate([flux_one, flux_two], 0))
        ) + dot(abreast(flux_three), third_back)
    for k in (3, 4, 5):
        copies[k].wait()
    layer = lambda l: slice(l * rows, (l + 1) * rows)
    body = (modes - 1) * rows
    up_layers = [
        (0, rows, lp_ref[layer(layers - modes), :]),
        (rows, 2 * rows, lp_ref[layer(layers - modes + 1), :] + lp_ref[layer(layers - modes + 2), :]),
        (2 * rows, body, lp_ref[(layers - modes + 3) * rows :, :]),
    ]
    down_layers = [
        (0, body - 2 * rows, lp_ref[: (modes - 3) * rows, :]),
        (body - 2 * rows, body - rows, lp_ref[layer(modes - 3), :] + lp_ref[layer(modes - 2), :]),
        (body - rows, body, lp_ref[layer(modes - 1), :]),
    ]
    forward = even(lax.axis_index("stream"))

    def fill(ref, parts, a):
        for begin, end, value in parts:
            ref[begin:end, :] = value
        ref[body:, :] = jnp.zeros((rows, width), F32)
        ref[body:, :modes] = mf_ref[:rows, a, :]
        ref[body : body + modes - rows, 16 : 16 + modes] = mf_ref[rows:, a, :]
        ref[body : body + 1, 32 : 32 + modes] = ef_ref[a : a + 1, :]

    @pl.when(forward)
    def _():
        fill(near_ref, up_layers, first_blocks - 1)
        fill(far_ref, down_layers, 0)

    @pl.when(jnp.logical_not(forward))
    def _():
        fill(near_ref, down_layers, 0)
        fill(far_ref, up_layers, first_blocks - 1)


def from_sides(near, far, axis):
    index = lax.axis_index(axis)
    is_even = even(index)
    before = jnp.where(is_even, far, near)
    after = jnp.where(is_even, near, far)
    before = jnp.where(index == 0, 0.0, before)
    after = jnp.where(index == lax.axis_size(axis) - 1, 0.0, after)
    return before, after


def lane_masks(width):
    lane = lax.broadcasted_iota(jnp.int32, (1, width), 1)
    node = over(lane, N1)[1]
    return lane, node, (node == 0) & (lane > 0)


def pack(upper_ref, lower_ref, spare):
    width = spare.shape[1]
    lane, node, free = lane_masks(width)
    final = (node == N1 - 1) & (lane < width - 1)
    upper = lax.broadcasted_iota(jnp.int32, (N1, 1), 0) < N1 // 2
    hidden = [jnp.where(lane == N1, pltpu.roll(spare, N1, 1), 0.0)]
    hidden += [pltpu.roll(spare, N1 - j, 1) for j in range(1, N1)]
    hidden[N1 - 1] = hidden[N1 - 1] + spare
    last = jnp.zeros_like(spare)
    for j in range(1, N1):
        last = jnp.where(lane == N1 * j, pltpu.roll(spare, N1 + (N1 - 1) * j, 1), last)
    hidden.append(last)
    for ref, mine in ((upper_ref, upper), (lower_ref, jnp.logical_not(upper))):
        value = ref[...]
        value = value + jnp.where(final, pltpu.roll(value, width - 1, 1), 0.0)
        for j in range(ref.shape[0] // N1):
            here = slice(j * N1, (j + 1) * N1)
            ref[here, :] = jnp.where(free & mine, hidden[min(j, N1)], jnp.where(free, 0.0, value[here]))


def unpack_spare(upper_rows, lower_rows):
    width = upper_rows.shape[1]
    lane, node, _ = lane_masks(width)
    upper = lax.broadcasted_iota(jnp.int32, (N1, 1), 0) < N1 // 2
    tiles = []
    for j in range(N1 + 1):
        here = slice(j * N1, (j + 1) * N1)
        tiles.append(jnp.where(upper, upper_rows[here], lower_rows[here]))
    spare = jnp.zeros((N1, width), F32)
    for j in range(N1):
        spare = jnp.where((node == j) & (lane < width - N1), pltpu.roll(tiles[j], width - N1 + j, 1), spare)
    for j in range(1, N1):
        spare = jnp.where(
            lane == width - N1 + j, pltpu.roll(tiles[N1], width - N1 - (N1 - 1) * j, 1), spare
        )
    return spare


def unpack(upper_rows, lower_rows, out_upper_ref, out_lower_ref):
    width = upper_rows.shape[1]
    free = lane_masks(width)[2]
    spare = unpack_spare(upper_rows, lower_rows)
    inner = upper_rows.shape[0] // 2
    padded = out_upper_ref.shape[0] // 2
    for ref, packed, start in ((out_upper_ref, upper_rows, 0), (out_lower_ref, lower_rows, N1 // 2)):
        value = jnp.where(free, 0.0, packed)
        for slot in range(2):
            base, row = slot * padded, start + 2 * slot
            ref[base : base + 1, :] = spare[row : row + 1]
            ref[base + 1 : base + 1 + inner, :] = value[slot * inner : (slot + 1) * inner]
            ref[base + 1 + inner : base + 2 + inner, :] = spare[row + 1 : row + 2]
            ref[base + 2 + inner : base + padded, :] = jnp.zeros((padded - inner - 2, width), F32)


def rows_kernel(lp_ref, near_ref, far_ref, built_ref, out_far_ref, out_near_ref):
    rows = N1
    layers = lp_ref.shape[0] // rows
    count = N1 + 1
    inner = out_near_ref.shape[0] // 2
    found = {}
    for k in (0, 1, rows - 2, rows - 1):
        before, after = from_sides(
            near_ref[pl.ds(k, count, stride=rows), :], far_ref[pl.ds(k, count, stride=rows), :], "stream"
        )
        found[k] = (before, lp_ref[pl.ds(k, layers, stride=rows), :], after)
    up = even(lax.axis_index("cross"))
    spare = []
    for ref, high in ((out_near_ref, up), (out_far_ref, jnp.logical_not(up))):
        for slot in range(2):
            base = slot * inner
            before, own, after = [
                jnp.where(high, one, two) for one, two in zip(found[rows - 2 + slot], found[slot])
            ]
            spare += [before[:1], after[count - 1 :]]
            ref[base : base + count - 2, :] = before[1 : count - 1]
            base += count - 2
            for l in range(0, layers, N1):
                previous = before[count - 1 :] if l == 0 else own[l - 1 : l]
                ref[base : base + 1, :] = previous + own[l : l + 1]
                ref[base + 1 : base + N1 - 1, :] = own[l + 1 : l + N1 - 1]
                base += N1 - 1
            ref[base : base + 1, :] = own[layers - 1 :] + after[:1]
            ref[base + 1 : base + count - 1, :] = after[1 : count - 1]
    pack(out_near_ref, out_far_ref, jnp.concatenate(spare, 0))


def spread_columns(parts, lay, pick):
    table = dot(parts, lay, ((0,), (0,)))
    return dot(pick, jnp.concatenate(split3(table), 0))


def spread_rows(parts, pick, rows):
    pad = parts.shape[0] // 3
    table = sum(dot(parts[k * pad : (k + 1) * pad], pick) for k in range(3))
    return dot(rows, jnp.concatenate(split3(table), 0))


def halves_by_lane(value, low):
    high = value.astype(BF16).astype(F32)
    return jnp.where(low, value - high, high).astype(BF16)


def low_lanes(kin, rim):
    lane = lax.broadcasted_iota(jnp.int32, (1, 3 * (kin + rim)), 1)
    return ((lane >= 2 * kin) & (lane < 3 * kin)) | (lane >= 3 * kin + 2 * rim)


def low_back_lanes(pairs):
    return lax.broadcasted_iota(jnp.int32, (1, 3 * pairs), 1) >= 2 * pairs


def ramps(*dims):
    return [lax.broadcasted_iota(jnp.int32, dims, axis) for axis in range(2)]


def over(value, count):
    if count & (count - 1) == 0:
        return lax.shift_right_logical(value, count.bit_length() - 1), value & (count - 1)
    quotient = ((value.astype(F32) + 0.5) * (1.0 / count)).astype(jnp.int32)
    return quotient, value - quotient * count


def mask(hit):
    return jnp.where(hit, 1.0, 0.0).astype(BF16)


def spread_table(blocks, modes):
    row, column = ramps(modes, blocks * modes)
    return mask(row == over(column, modes)[1])


def gather_table(blocks, modes):
    row, column = ramps(blocks * N1, modes * blocks)
    node, block = over(column, blocks)
    place = row - block * N1
    hit = (place == node - 1) & (node >= 1) & (node <= N1)
    for n, at in ((0, -2), (1, -1), (N1, N1), (N1 + 1, N1 + 1)):
        hit = hit | ((node == n) & (place == at))
    return mask(hit)


def pick_table(pairs, pad, modes, which):
    row, column = ramps(pairs, 3 * pad)
    return mask(over(row, modes)[which] == over(column, pad)[1])


def pick_rows(pairs, pad, modes, which):
    row, column = ramps(pairs, pad)
    return jnp.where(over(row, modes)[which] == column, 1.0, 0.0)


def back_tables(pairs, pad, modes):
    row, column = ramps(pad, 3 * pairs)
    found = over(over(column, pairs)[1], modes)
    return mask(found[0] == row), mask(found[1] == row)


def box_rows(count, pad):
    row, column = ramps(count, 3 * pad)
    first, second = over(row, N1)
    column = over(column, pad)[1]
    return mask(first + 1 == column), mask(second + 1 == column)


def face_rows(pad):
    row, column = ramps(2 * N1, 3 * pad)
    face, first = over(row, N1)
    column = over(column, pad)[1]
    return mask(first + 1 == column), mask(jnp.where(face == 0, 1, N1) == column)


def inner_table(blocks, modes):
    row, column = ramps(modes * blocks, blocks * N1)
    node, block = over(row, blocks)
    place = column - block * N1
    hit = (place == node - 1) & (node >= 1) & (node <= N1)
    return mask(hit | ((node == 1) & (place == -1)) | ((node == N1) & (place == N1)))


def lay_tables(pad, kin, rim):
    layers = kin // N1
    row, column = ramps(3 * pad, 3 * (kin + rim))
    row = over(row, pad)[1]
    own = column < 3 * kin
    l_own, y = over(over(column, kin)[1], N1)
    kind, l_rim = over(over(jnp.maximum(column - 3 * kin, 0), rim)[1], rim // 4)
    node = jnp.where(l_own == 0, 0, jnp.where(l_own == layers - 1, N1 + 1, jnp.clip(l_own - 1, 1, N1)))
    node = jnp.where(own, node, l_rim)
    second = jnp.where(own, y + 1, jnp.where(kind < 2, kind, N1 - 2 + kind))
    inside = own | (l_rim < N1 + 2)
    return mask(inside & (row == node)), mask(inside & (row == second))


def third_parts(mt_ref, spread):
    rows, modes = mt_ref.shape
    blocks = rows // modes
    row, column = ramps(rows, rows)
    own = over(row, blocks)[1] == over(column, modes)[0]
    return [jnp.where(own, dot(part, spread), 0.0).astype(BF16) for part in split3(mt_ref[...])]


def pad_modes(pad_ref, mf_ref, ms_ref):
    modes = ms_ref.shape[0]
    first_blocks = pad_ref.shape[0] - 1
    pad_ref[...] = jnp.zeros_like(pad_ref)
    for a in range(first_blocks):
        pad_ref[a, :modes, :modes] = mf_ref[:, a, :]
    pad_ref[first_blocks, :modes, :modes] = ms_ref[:, 0, :]


def modes_kernel(
    mt_ref, e3_ref, mf_ref, ef_ref, ms_ref, es_ref,
    w_ref, e3_row_ref, own_columns_ref, own_rim_ref, second_columns_ref, pad_ref, eigen_ref, back_ref,
):
    blocks, modes = e3_ref.shape
    spread = spread_table(blocks, modes)
    gather = gather_table(blocks, modes)
    table = sum(dot(gather, part) for part in third_parts(mt_ref, spread))
    high, low = split(table)
    w_ref[...] = jnp.concatenate([high, low, high], 0)
    row, column = ramps(blocks, blocks * modes)
    e3_wide = sum(dot(part, spread) for part in split3(e3_ref[...]))
    e3_row_ref[...] = jnp.sum(
        jnp.where(row == over(column, modes)[0], e3_wide, 0.0), 0, keepdims=True
    )
    first_blocks, pairs, kin = own_columns_ref.shape
    kin, rim, pad = kin // 3, own_rim_ref.shape[2] // 3, pad_ref.shape[1]
    pad_modes(pad_ref, mf_ref, ms_ref)
    eigen_ref[...] = jnp.zeros_like(eigen_ref)
    eigen_ref[:first_blocks, :modes] = ef_ref[...]
    eigen_ref[first_blocks : first_blocks + 1, :modes] = es_ref[...]
    lay_m, lay_n = lay_tables(pad, kin, rim)
    low = low_lanes(kin, rim)
    second = jnp.concatenate(split3(pad_ref[first_blocks]), 0)
    second_columns = spread_columns(second, lay_n, pick_table(pairs, pad, modes, 1))
    second_columns_ref[...] = second_columns
    pick = pick_table(pairs, pad, modes, 0)
    for a in range(first_blocks):
        first = jnp.concatenate(split3(pad_ref[a]), 0)
        columns = halves_by_lane(spread_columns(first, lay_m, pick) * second_columns, low)
        own_columns_ref[a] = columns[:, : 3 * kin]
        own_rim_ref[a] = columns[:, 3 * kin :]
    box = back_ref.shape[1]
    back_m, back_n = back_tables(pairs, pad, modes)
    rows_m, rows_n = box_rows(box, pad)
    second_rows = spread_rows(second, back_n, rows_n)
    for a in range(first_blocks):
        first = jnp.concatenate(split3(pad_ref[a]), 0)
        back_ref[a] = halves_by_lane(spread_rows(first, back_m, rows_m) * second_rows, low_back_lanes(pairs))


def columns_kernel(
    lp_ref, near_ref, far_ref, w_ref, e3_row_ref, own_columns_ref, second_columns_ref, pad_ref,
    eigen_ref, mt_ref, v_ref, side_rim_ref, rec_ref, face_ref, wbh_ref, wbl_ref,
):
    rows = N1
    halo = (N1 + 2) * rows
    first_blocks, pairs, kin = own_columns_ref.shape
    kin, rim, pad, modes = kin // 3, side_rim_ref.shape[2] // 3, pad_ref.shape[1], N1 + 2
    box = N1 * rows
    near, far = near_ref[...], far_ref[...]
    before, after = from_sides(near, far, "stream")
    odd = jnp.logical_not(even(lax.axis_index("stream")))
    body = halo - rows
    zero = jnp.zeros((rows, lp_ref.shape[1]), F32)
    stack = jnp.concatenate(
        [before[:rows], zero, before[rows:body], lp_ref[...], after[: body - rows], zero, after[body - rows : body]], 0
    )
    u = dot(abreast(stack), w_ref[...])
    edge_near, edge_far = near[body : body + 1, 32 : 32 + pad], far[body : body + 1, 32 : 32 + pad]
    low = low_lanes(kin, rim)
    lay_m, _ = lay_tables(pad, kin, rim)
    pick_p3 = pick_table(pairs, pad, modes, 0)
    pick_p, pick_q = pick_rows(pairs, pad, modes, 0), pick_rows(pairs, pad, modes, 1)
    back_m, back_n = back_tables(pairs, pad, modes)
    face_m, face_n = face_rows(pad)
    own_eigen = eigen_ref[...]
    firsts = [jnp.concatenate([side[body:, :pad], side[body:, 16 : 16 + pad]], 0) for side in (before, after)]
    firsts = [firsts[0]] + [pad_ref[a] for a in range(first_blocks)] + [firsts[1]]
    eigens = [jnp.where(odd, edge_near, edge_far)] + [own_eigen[a : a + 1] for a in range(first_blocks)]
    eigens += [jnp.where(odd, edge_far, edge_near)]
    second = jnp.concatenate(split3(pad_ref[first_blocks]), 0)
    second_faces = spread_rows(second, back_n, face_n)
    second_sum = jnp.sum(pick_q * own_eigen[first_blocks : first_blocks + 1], 1, keepdims=True)
    for a, (first, eigen) in enumerate(zip(firsts, eigens)):
        first = jnp.concatenate(split3(first), 0)
        if a in (0, first_blocks + 1):
            columns = halves_by_lane(
                spread_columns(first, lay_m, pick_p3) * second_columns_ref[...], low
            )
            side_rim_ref[min(a, 1)] = columns[:, 3 * kin :]
            columns = columns[:, : 3 * kin]
        else:
            columns = own_columns_ref[a - 1]
        begin = a * box
        v_ref[a] = dot(columns, stacked(u[begin : begin + kin]))
        high, low_half = split((spread_rows(first, back_m, face_m) * second_faces)[:, :pairs])
        face_ref[a] = jnp.concatenate([high, low_half], 0)
        total = jnp.sum(pick_p * eigen, 1, keepdims=True) + second_sum
        rec_ref[a] = 1.0 / (total + e3_row_ref[...])
    blocks = mt_ref.shape[0] // modes
    inner = inner_table(blocks, modes)
    table = sum(
        dot(part, inner, ((0,), (0,))) for part in third_parts(mt_ref, spread_table(blocks, modes))
    )
    wbh_ref[...], wbl_ref[...] = split(table)


def spectral_columns(near, far, w_ref, v_ref, own_rim_ref, side_rim_ref, rec_ref):
    columns = v_ref.shape[0]
    inner = near.shape[0] // 2
    half = N1 // 2
    free = lane_masks(near.shape[1])[2]
    spare = unpack_spare(near, far)
    before, after = from_sides(jnp.where(free, 0.0, near), jnp.where(free, 0.0, far), "cross")
    ends = jnp.concatenate(from_sides(spare[:half], spare[half:], "cross"), 0)
    u = dot(abreast(jnp.concatenate([before, after, ends], 0)), w_ref[...])
    found = []
    for a in range(columns):
        rim = []
        for k in range(4):
            base, end = k * inner, 4 * inner + 2 * k
            start = a * (N1 - 1) - 1
            if a == 0:
                rim += [u[end : end + 1], u[base : base + 15]]
            elif a == columns - 1:
                count = inner - start
                rim += [u[base + start : base + inner], u[end + 1 : end + 2]]
                rim += [jnp.zeros((15 - count, u.shape[1]), F32)]
            else:
                rim += [u[base + start : base + start + 16]]
        rim = jnp.concatenate(rim, 0)
        table = side_rim_ref[min(a, 1)] if a in (0, columns - 1) else own_rim_ref[a - 1]
        found.append((v_ref[a] + dot(table, stacked(rim))) * rec_ref[a])
    return found


def third_back(parts, wbh_ref, wbl_ref):
    high, low = split(jnp.concatenate(parts, 0))
    count, width = high.shape[0], wbh_ref.shape[1]
    both = dot(jnp.concatenate([high, low], 0), jnp.concatenate([wbh_ref[...], wbl_ref[...]], 1))
    return both[:count, :width] + both[count:, :width] + both[:count, width:]


def faces_kernel(
    far_ref, near_ref, w_ref, v_ref, own_rim_ref, side_rim_ref, rec_ref, wbh_ref, wbl_ref, face_ref,
    out_far_ref, out_near_ref, spectral_ref,
):
    rows = N1
    found = spectral_columns(near_ref[...], far_ref[...], w_ref, v_ref, own_rim_ref, side_rim_ref, rec_ref)
    columns = len(found)
    for a in range(columns):
        spectral_ref[a] = found[a]
    parts = []
    for a in range(columns):
        high, low = split(found[a])
        both = dot(face_ref[a], high)
        parts.append(both[: 2 * N1] + both[2 * N1 :] + dot(face_ref[a, : 2 * N1], low))
    solved = third_back(parts, wbh_ref, wbl_ref)
    row = lax.broadcasted_iota(jnp.int32, (rows, 1), 0)
    up = even(lax.axis_index("cross"))
    for a in range(1, columns - 1):
        sums = []
        for face in range(2):
            base = 16 * a + rows * face
            previous = base - 16 + rows - 1
            after = base + 16
            sums.append(
                solved[base : base + rows]
                + jnp.where(row == 0, solved[previous : previous + 1], 0.0)
                + jnp.where(row == rows - 1, solved[after : after + 1], 0.0)
            )
        here = slice((a - 1) * rows, a * rows)
        out_near_ref[here, :] = jnp.where(up, sums[1], sums[0])
        out_far_ref[here, :] = jnp.where(up, sums[0], sums[1])


def assemble_operator(lp_ref, s_near_ref, s_far_ref, c_near_ref, c_far_ref, out_ref, acc_ref):
    rows = N1
    total_rows, width = lp_ref.shape
    padded = c_near_ref.shape[0] // 2
    body = (N1 + 1) * rows
    box = N1 * rows
    before, after = from_sides(s_near_ref[...], s_far_ref[...], "stream")
    left, right = from_sides(c_near_ref[...], c_far_ref[...], "cross")
    acc_ref[...] = lp_ref[...]
    for base in range(0, total_rows, box):
        last = base + box
        previous = before[body - rows : body] if base == 0 else lp_ref[base - rows : base, :]
        following = after[:rows] if last == total_rows else lp_ref[last : last + rows, :]
        acc_ref[base : base + rows, :] = lp_ref[base : base + rows, :] + previous
        acc_ref[last - rows : last, :] = lp_ref[last - rows : last, :] + following
        node = (N1 - 1) * (base // box + 1) + 1
        low, high = pl.ds(base, N1, stride=rows), pl.ds(base + rows - 1, N1, stride=rows)
        acc_ref[low, :] = acc_ref[low, :] + left[padded + node : padded + node + N1]
        acc_ref[high, :] = acc_ref[high, :] + right[node : node + N1]
    lane = lax.broadcasted_iota(jnp.int32, (1, width), 1)
    first = (lax.rem(lane, N1) == 0) & (lane > 0)
    final = (lax.rem(lane, N1) == N1 - 1) & (lane < width - 1)
    value = acc_ref[...]
    value = (
        value
        + jnp.where(first, pltpu.roll(value, 1, 1), 0.0)
        + jnp.where(final, pltpu.roll(value, width - 1, 1), 0.0)
    )
    out_ref[...] = value.reshape(out_ref.shape)


def solve_kernel(
    lp_ref, s_near_ref, s_far_ref, c_far_ref, c_near_ref, spectral_ref, wbh_ref, wbl_ref, pad_ref, back_ref,
    operator_ref, r_ref, out_ref, acc_ref, all_near_ref, all_far_ref, sem,
):
    unpack(c_near_ref[...], c_far_ref[...], all_near_ref, all_far_ref)
    assemble_operator(lp_ref, s_near_ref, s_far_ref, all_near_ref, all_far_ref, out_ref, acc_ref)
    copy = pltpu.make_async_copy(out_ref, operator_ref, sem)
    copy.start()
    rows = N1
    box = N1 * rows
    found = [spectral_ref[a] for a in range(spectral_ref.shape[0])]
    columns = len(found)
    pad, pairs = pad_ref.shape[1], spectral_ref.shape[1]
    back_m, back_n = back_tables(pairs, pad, N1 + 2)
    rows_m, rows_n = box_rows(box, pad)
    low = low_back_lanes(pairs)
    body = (N1 + 1) * rows
    sides = from_sides(s_near_ref[...], s_far_ref[...], "stream")
    sides = [jnp.concatenate([side[body:, :pad], side[body:, 16 : 16 + pad]], 0) for side in sides]
    second = jnp.concatenate(split3(pad_ref[columns - 2]), 0)
    parts = [None] * columns
    for a, first, kept in ((0, sides[0], slice(box - 16, box)), (columns - 1, sides[1], slice(0, 16))):
        first = jnp.concatenate(split3(first), 0)
        table = spread_rows(first, back_m, rows_m[kept]) * spread_rows(second, back_n, rows_n[kept])
        parts[a] = dot(halves_by_lane(table, low), stacked(found[a]))
    for a in range(1, columns - 1):
        parts[a] = dot(back_ref[a - 1], stacked(found[a]))
    parts[0] = parts[0][16 - rows :]
    parts[-1] = parts[-1][:rows]
    solved = third_back(parts, wbh_ref, wbl_ref)
    for a in range(columns - 2):
        base = rows + a * box
        top, bottom = solved[base : base + rows], solved[base + box - rows : base + box]
        r_ref[a * box : a * box + rows, :] = top + solved[base - rows : base]
        r_ref[a * box + rows : (a + 1) * box - rows, :] = solved[base + rows : base + box - rows]
        r_ref[(a + 1) * box - rows : (a + 1) * box, :] = bottom + solved[base + box : base + box + rows]
    copy.wait()


def pass_kernel(*refs):
    count = len(refs) // 2
    for source, target in zip(refs[:count], refs[count:]):
        target[...] = source[...]


def add_kernel(r_ref, ahead_ref, far_ref, near_ref, out_ref, acc_ref, sem):
    rows = N1
    near = jnp.where(lax.axis_index("cross") < 2, ahead_ref[...], near_ref[...])
    before, after = from_sides(near, far_ref[...], "cross")
    row = lax.broadcasted_iota(jnp.int32, (rows, 1), 0)
    for l in range(acc_ref.shape[0]):
        value = r_ref[l * rows : (l + 1) * rows, :] + jnp.where(row == 0, before[l : l + 1], 0.0)
        acc_ref[l] = value + jnp.where(row == rows - 1, after[l : l + 1], 0.0)
    copy = pltpu.make_async_copy(acc_ref, out_ref, sem)
    copy.start()
    copy.wait()


def shape(*dims, dtype=F32):
    return pltpu.VMEM(dims, dtype)


def call(kernel, name, out, *args, scratch=(), out_specs=None, flops=1000000, place=pltpu.VMEM):
    single = not isinstance(out, list)
    args = [pltpu.with_memory_space_constraint(x, place) for x in args]
    return pl.pallas_call(
        kernel,
        out_shape=out,
        in_specs=[pl.BlockSpec(memory_space=place)] * len(args),
        out_specs=out_specs if out_specs is not None else (VMEM if single else [VMEM] * len(out)),
        scratch_shapes=list(scratch),
        compiler_params=pltpu.CompilerParams(vmem_limit_bytes=VMEM_LIMIT),
        cost_estimate=pl.CostEstimate(flops=flops, bytes_accessed=flops, transcendentals=0),
        name=name,
    )(*args)


def swaps(axis):
    count = lax.axis_size(axis)
    near = [(i, i ^ 1) for i in range(count)]
    far = [(i, (i - 1) % count if i % 2 == 0 else (i + 1) % count) for i in range(count)]
    return near, far


def swap_stream(near, far):
    first, second = swaps("stream")
    near = lax.ppermute(near, "stream", first)
    far = lax.ppermute(far, "stream", second)
    return near, far


def cross_pairs(near, ahead=None):
    count, streams = lax.axis_size("cross"), lax.axis_size("stream")
    pairs = []
    for s in range(streams):
        for i in range(count):
            j = i ^ 1 if near else i - 1 + 2 * (i % 2)
            idle = not 0 <= j < count or (ahead is not None and (i < 2) != ahead)
            pairs.append((s * count + i, (s ^ 1) * count + i if idle else s * count + j))
    return pairs


def swap_cross(near, far):
    axes = ("stream", "cross")
    return lax.ppermute(near, axes, cross_pairs(True)), lax.ppermute(far, axes, cross_pairs(False))


def swap_cross_ahead(near, far):
    axes = ("stream", "cross")
    first = lax.ppermute(near, axes, cross_pairs(True, True))
    far, near = call(pass_kernel, "pass_on", [shape(*far.shape), shape(*near.shape)], far, near)
    return first, lax.ppermute(far, axes, cross_pairs(False)), lax.ppermute(near, axes, cross_pairs(True, False))


def shards(
    pressure, geo_diag, geo_off, modes_first, modes_second, modes_third, eigen_first, eigen_second,
    eigen_third,
):
    layers, rows, width = pressure.shape
    modes = modes_first.shape[1]
    if layers < 3 * N1 or rows != N1 or modes != N1 + 2 or lax.axis_size("stream") % 2 or lax.axis_size("cross") % 2:
        raise ValueError("unsupported sizes")
    first_blocks, third_blocks = layers // N1, width // N1
    columns = first_blocks + 2
    halo = modes * rows
    box = N1 * rows
    nodes = (first_blocks + 1) * (N1 - 1) + modes
    padded = round_up(nodes, 8)
    wide = third_blocks * modes

    pairs, pad = round_up(modes * modes, 16), round_up(modes, 16)

    mf = jnp.transpose(modes_first, (1, 0, 2))
    ms = jnp.transpose(modes_second, (1, 0, 2))
    mt = jnp.transpose(modes_third, (1, 0, 2)).reshape(modes * third_blocks, modes)

    inputs = [pressure, geo_diag, geo_off, mf, eigen_first, eigen_second]
    lp, s_near, s_far, mf, ef, es = call(
        local_kernel, "local_product",
        [
            shape(layers * rows, width), shape(halo, width), shape(halo, width),
            shape(modes, first_blocks, modes), shape(first_blocks, modes), shape(1, modes),
        ],
        *inputs, place=pltpu.HBM,
        scratch=[pltpu.VMEM(x.shape, x.dtype) for x in inputs[:3]] + [pltpu.SemaphoreType.DMA((len(inputs),))],
    )
    s_near, s_far = swap_stream(s_near, s_far)
    kin, rim_width = 3 * (N1 + 4) * rows, 3 * 64
    w, e3_row, own_columns, own_rim, second_columns, padded_modes, eigen, own_back = call(
        modes_kernel, "mode_tables",
        [
            shape(3 * width, wide, dtype=BF16), shape(1, wide),
            shape(first_blocks, pairs, kin, dtype=BF16), shape(first_blocks, pairs, rim_width, dtype=BF16),
            shape(pairs, kin + rim_width), shape(first_blocks + 1, pad, pad), shape(first_blocks + 1, pad),
            shape(first_blocks, box, 3 * pairs, dtype=BF16),
        ],
        mt, eigen_third, mf, ef, ms, es,
    )
    c_far, c_near = call(
        rows_kernel, "rows_to_send",
        [shape(2 * nodes - 4, width), shape(2 * nodes - 4, width)],
        lp, s_near, s_far, e3_row,
    )
    c_near, c_far = swap_cross(c_near, c_far)
    v, side_rim, rec, face, wbh, wbl = call(
        columns_kernel, "own_part",
        [
            shape(columns, pairs, wide), shape(2, pairs, rim_width, dtype=BF16), shape(columns, pairs, wide),
            shape(columns, 4 * N1, pairs, dtype=BF16), shape(wide, width, dtype=BF16), shape(wide, width, dtype=BF16),
        ],
        lp, s_near, s_far, w, e3_row, own_columns, second_columns, padded_modes, eigen, mt,
    )
    f_far, f_near, spectral = call(
        faces_kernel, "faces",
        [
            shape(layers, width), shape(layers, width), shape(columns, pairs, wide),
        ],
        c_far, c_near, w, v, own_rim, side_rim, rec, wbh, wbl, face,
    )
    f_ahead, f_far, f_near = swap_cross_ahead(f_near, f_far)
    result = pltpu.HBM(pressure.shape, F32)
    in_hbm = pl.BlockSpec(memory_space=pltpu.HBM)
    operator_out, restricted = call(
        solve_kernel, "solve", [result, shape(layers * rows, width)],
        lp, s_near, s_far, c_far, c_near, spectral, wbh, wbl, padded_modes, own_back, out_specs=[in_hbm, VMEM],
        scratch=[
            pltpu.VMEM(pressure.shape, F32), pltpu.VMEM((layers * rows, width), F32),
            pltpu.VMEM((2 * padded, width), F32), pltpu.VMEM((2 * padded, width), F32), pltpu.SemaphoreType.DMA,
        ],
    )
    preconditioned = call(
        add_kernel, "preconditioned", result, restricted, f_ahead, f_far, f_near, out_specs=in_hbm,
        scratch=[pltpu.VMEM(pressure.shape, F32), pltpu.SemaphoreType.DMA],
    )
    return (operator_out, preconditioned)


def solution(mesh):
    in_specs = (
        P("stream", "cross", None),
        P(None, "stream", "cross", None),
        P(None, "stream", "cross", None),
        P("stream", None, None),
        P("cross", None, None),
        P(),
        P("stream", None),
        P("cross", None),
        P(),
    )
    out_specs = (P("stream", "cross", None), P("stream", "cross", None))
    return jax.shard_map(shards, mesh=mesh, in_specs=in_specs, out_specs=out_specs, check_vma=False)
```

profile of v0, /device:TPU:18, one launch (start us, length us, event | category | flops | bytes accessed | tf_op | source)
XLA Modules:
  0.0 18.4 jit_solution(2394719669087555143)
XLA Ops:
  0.6 0.0 copy-start
  0.6 1.6 %local_product.1 = (f32[192,128]{1,0:T(8,128)S(1)}, f32[80,128]{1,0:T(8,128)S(1)}, f32[80,128]{1,0:T(8,128)S(1)}, f32[10,3,10]{2,1,0:T(4,128)S(1)}, f32[3,10]{1,0:T(4,128)S(1)}, /*index=5*/f32[1,10]{1,0:T(1,128)S(1)}) custom-call(f32[24,8,128]{2,1,0:T(8,128)} %refs_0_.1, f32[3,24,8,128]{3,2,1,0:T(8,128)} %refs_1_.1, f32[3,24,8,128]{3,2,1,0:T(8,128)} %refs_2_.1, ...), custom_call_target="tpu_custom_call" | custom-call | flops 1000000 | bytes 1000000 | tf_op jit(solution)/shard_map/local_product/pallas_call | solution.py:694
  2.2 0.0 copy-start.1
  2.2 0.1 collective-permute-start
  2.3 0.0 copy-start.2
  2.3 1.6 %collective-permute-start.1 = (f32[80,128]{1,0:T(8,128)S(1)}, f32[80,128]{1,0:T(8,128)S(1)}, u32[]{:S(2)}, u32[]{:S(2)}) collective-permute-start(f32[80,128]{1,0:T(8,128)S(1)} %get-tuple-element.33), channel_id=1, source_target_pairs={{0,24},{8,16},{16,8},{24,0},{1,25},{9,17},{17,9},{25,1},{2,26},{10... | collective-permute-start | bytes 122888 | tf_op jit(solution)/shard_map/ppermute | solution.py:716
  3.9 0.0 copy-done
  3.9 0.0 copy-done.1
  3.9 0.0 copy-done.2
  3.9 1.3 %mode_tables.1 = (bf16[384,160]{1,0:T(8,128)(2,1)S(1)}, f32[1,160]{1,0:T(1,128)S(1)}, bf16[3,112,288]{2,1,0:T(8,128)(2,1)S(1)}, bf16[3,112,192]{2,1,0:T(8,128)(2...) custom-call(f32[160,10]{1,0:T(8,128)S(1)} %bitcast.5, ...), custom_call_target="tpu_custom_call" | custom-call | flops 1000000 | bytes 1000000 | tf_op jit(solution)/shard_map/mode_tables/pallas_call | solution.py:694
  5.3 0.0 collective-permute-done.near_ref.s_near_ref
  5.3 0.5 %collective-permute-done.1.far_ref.s_far_ref = f32[80,128]{1,0:T(8,128)S(1)} collective-permute-done((f32[80,128]{1,0:T(8,128)S(1)}, f32[80,128]{1,0:T(8,128)S(1)}, u32[]{:S(2)}, u32[]{:S(2)}) %collective-permute-start.1) | collective-permute-done | bytes 40992 | tf_op jit(solution)/shard_map/ppermute | solution.py:716
  5.8 0.1 rows_to_send.1
  5.9 1.6 %collective-permute-start.2 = (f32[72,128]{1,0:T(8,128)S(1)}, f32[72,128]{1,0:T(8,128)S(1)}, u32[]{:S(2)}, u32[]{:S(2)}) collective-permute-start(f32[72,128]{1,0:T(8,128)S(1)} %get-tuple-element.38), channel_id=1, source_target_pairs={{0,8},{1,2},{2,1},{3,4},{4,3},{5,6},{6,5},{7,15},{8,0},{9,10},{10,... | collective-permute-start | bytes 110600 | tf_op jit(solution)/shard_map/ppermute | solution.py:733
  7.5 0.4 %collective-permute-start.3 = (f32[72,128]{1,0:T(8,128)S(1)}, f32[72,128]{1,0:T(8,128)S(1)}, u32[]{:S(2)}, u32[]{:S(2)}) collective-permute-start(f32[72,128]{1,0:T(8,128)S(1)} %get-tuple-element.39), channel_id=1, source_target_pairs={{0,1},{1,0},{2,3},{3,2},{4,5},{5,4},{6,7},{7,6},{8,9},{9,8},{10,11... | collective-permute-start | bytes 110600 | tf_op jit(solution)/shard_map/ppermute | solution.py:733
  7.9 1.7 %own_part.1 = (f32[5,112,160]{2,1,0:T(8,128)S(1)}, bf16[2,112,192]{2,1,0:T(8,128)(2,1)S(1)}, f32[5,112,160]{2,1,0:T(8,128)S(1)}, bf16[5,32,112]{2,1,0:T(8,128)(2...) custom-call(f32[192,128]{1,0:T(8,128)S(1)} %get-tuple-element.31.lp_ref, ...), custom_call_target="tpu_custom_call" | custom-call | flops 1000000 | bytes 1000000 | tf_op jit(solution)/shard_map/own_part/pallas_call | solution.py:694
  9.6 1.3 %collective-permute-done.2.far_ref.c_far_ref = f32[72,128]{1,0:T(8,128)S(1)} collective-permute-done((f32[72,128]{1,0:T(8,128)S(1)}, f32[72,128]{1,0:T(8,128)S(1)}, u32[]{:S(2)}, u32[]{:S(2)}) %collective-permute-start.2) | collective-permute-done | bytes 36896 | tf_op jit(solution)/shard_map/ppermute | solution.py:733
  10.9 0.6 %collective-permute-done.3.near_ref.c_near_ref = f32[72,128]{1,0:T(8,128)S(1)} collective-permute-done((f32[72,128]{1,0:T(8,128)S(1)}, f32[72,128]{1,0:T(8,128)S(1)}, u32[]{:S(2)}, u32[]{:S(2)}) %collective-permute-start.3) | collective-permute-done | bytes 36896 | tf_op jit(solution)/shard_map/ppermute | solution.py:733
  11.5 0.8 %faces.1 = (f32[24,128]{1,0:T(8,128)S(1)}, f32[24,128]{1,0:T(8,128)S(1)}, f32[5,112,160]{2,1,0:T(8,128)S(1)}) custom-call(f32[72,128]{1,0:T(8,128)S(1)} %collective-permute-done.2.far_ref.c_far_ref, f32[72,128]{1,0:T(8,128)S(1)} %collective-permute-done.3.near_ref.c_near_ref, bf16[384,160]{1,0:T(8,128)(2,1)S(1)} %get-tuple-element.40.w_ref, ...), custom_call_target="tpu_custom_call" | custom-call | flops 1000000 | bytes 1000000 | tf_op jit(solution)/shard_map/faces/pallas_call | solution.py:694
  12.3 0.1 collective-permute-start.4
  12.4 1.6 %collective-permute-start.5 = (f32[24,128]{1,0:T(8,128)S(1)}, f32[24,128]{1,0:T(8,128)S(1)}, u32[]{:S(2)}, u32[]{:S(2)}) collective-permute-start(f32[24,128]{1,0:T(8,128)S(1)} %get-tuple-element.58), channel_id=1, source_target_pairs={{0,8},{1,2},{2,1},{3,4},{4,3},{5,6},{6,5},{7,15},{8,0},{9,10},{10,... | collective-permute-start | bytes 36872 | tf_op jit(solution)/shard_map/ppermute | solution.py:740
  14.0 0.4 %collective-permute-start.6 = (f32[24,128]{1,0:T(8,128)S(1)}, f32[24,128]{1,0:T(8,128)S(1)}, u32[]{:S(2)}, u32[]{:S(2)}) collective-permute-start(f32[24,128]{1,0:T(8,128)S(1)} %get-tuple-element.59), channel_id=1, source_target_pairs={{0,8},{1,9},{2,3},{3,2},{4,5},{5,4},{6,7},{7,6},{8,0},{9,1},{10,11... | collective-permute-start | bytes 36872 | tf_op jit(solution)/shard_map/ppermute | solution.py:740
  14.4 1.6 %solve.1 = (f32[24,8,128]{2,1,0:T(8,128)}, f32[192,128]{1,0:T(8,128)S(1)}) custom-call(f32[192,128]{1,0:T(8,128)S(1)} %get-tuple-element.31.lp_ref, f32[80,128]{1,0:T(8,128)S(1)} %collective-permute-done.near_ref.s_near_ref, f32[80,128]{1,0:T(8,128)S(1)} %collective-permute-done.1.far_ref.s_far_ref, f32[72,128]{1,0:T(8,128)S(1)} %collective-permute-done.2.far_ref.c_far_ref, ...), custom_call_target="tpu_custom_call" | custom-call | flops 1000000 | bytes 1000000 | tf_op jit(solution)/shard_map/solve/pallas_call | solution.py:694
  16.0 0.0 collective-permute-done.4.ahead_ref
  16.0 1.1 %collective-permute-done.5.far_ref = f32[24,128]{1,0:T(8,128)S(1)} collective-permute-done((f32[24,128]{1,0:T(8,128)S(1)}, f32[24,128]{1,0:T(8,128)S(1)}, u32[]{:S(2)}, u32[]{:S(2)}) %collective-permute-start.5) | collective-permute-done | bytes 12320 | tf_op jit(solution)/shard_map/ppermute | solution.py:740
  17.1 0.7 %collective-permute-done.6.near_ref = f32[24,128]{1,0:T(8,128)S(1)} collective-permute-done((f32[24,128]{1,0:T(8,128)S(1)}, f32[24,128]{1,0:T(8,128)S(1)}, u32[]{:S(2)}, u32[]{:S(2)}) %collective-permute-start.6) | collective-permute-done | bytes 12320 | tf_op jit(solution)/shard_map/ppermute | solution.py:740
  17.7 0.7 %preconditioned.1 = f32[24,8,128]{2,1,0:T(8,128)} custom-call(f32[192,128]{1,0:T(8,128)S(1)} %get-tuple-element.55.r_ref, f32[24,128]{1,0:T(8,128)S(1)} %collective-permute-done.4.ahead_ref, f32[24,128]{1,0:T(8,128)S(1)} %collective-permute-done.5.far_ref, f32[24,128]{1,0:T(8,128)S(1)} %collective-permute-done.6.near_ref), custom_call_target="tpu_custom_call" | custom-call | flops 1000000 | bytes 1000000 | tf_op jit(solution)/shard_map/preconditioned/pallas_call | solution.py:694
  (1 shorter events, 0.0 us)
Async XLA Ops:
  0.6 3.3 %copy-start = (f32[16,10,10]{2,0,1:T(8,128)S(1)}, f32[16,10,10]{2,0,1:T(8,128)}, u32[]{:S(2)}) copy-start(f32[16,10,10]{2,0,1:T(8,128)} %param.14) | copy-start | bytes 19204
  2.2 1.7 %copy-start.1 = (f32[16,10]{1,0:T(8,128)S(1)}, f32[16,10]{1,0:T(8,128)}, u32[]{:S(2)}) copy-start(f32[16,10]{1,0:T(8,128)} %e3_ref.1) | copy-start | bytes 1924
  2.2 3.0 %collective-permute-start = (f32[80,128]{1,0:T(8,128)S(1)}, f32[80,128]{1,0:T(8,128)S(1)}, u32[]{:S(2)}, u32[]{:S(2)}) collective-permute-start(f32[80,128]{1,0:T(8,128)S(1)} %get-tuple-element.32), channel_id=1, source_target_pairs={{0,8},{8,0},{16,24},{24,16},{1,9},{9,1},{17,25},{25,17},{2,10},{10... | collective-permute-start | bytes 122888 | tf_op jit(solution)/shard_map/ppermute | solution.py:715
  2.3 1.6 %copy-start.2 = (f32[1,10,10]{2,0,1:T(1,128)S(1)}, f32[1,10,10]{2,0,1:T(1,128)}, u32[]{:S(2)}) copy-start(f32[1,10,10]{2,0,1:T(1,128)} %param.13) | copy-start | bytes 1204
  2.3 3.5 %collective-permute-start.1 = (f32[80,128]{1,0:T(8,128)S(1)}, f32[80,128]{1,0:T(8,128)S(1)}, u32[]{:S(2)}, u32[]{:S(2)}) collective-permute-start(f32[80,128]{1,0:T(8,128)S(1)} %get-tuple-element.33), channel_id=1, source_target_pairs={{0,24},{8,16},{16,8},{24,0},{1,25},{9,17},{17,9},{25,1},{2,26},{10... | collective-permute-start | bytes 122888 | tf_op jit(solution)/shard_map/ppermute | solution.py:716
  5.9 5.0 %collective-permute-start.2 = (f32[72,128]{1,0:T(8,128)S(1)}, f32[72,128]{1,0:T(8,128)S(1)}, u32[]{:S(2)}, u32[]{:S(2)}) collective-permute-start(f32[72,128]{1,0:T(8,128)S(1)} %get-tuple-element.38), channel_id=1, source_target_pairs={{0,8},{1,2},{2,1},{3,4},{4,3},{5,6},{6,5},{7,15},{8,0},{9,10},{10,... | collective-permute-start | bytes 110600 | tf_op jit(solution)/shard_map/ppermute | solution.py:733
  7.5 4.0 %collective-permute-start.3 = (f32[72,128]{1,0:T(8,128)S(1)}, f32[72,128]{1,0:T(8,128)S(1)}, u32[]{:S(2)}, u32[]{:S(2)}) collective-permute-start(f32[72,128]{1,0:T(8,128)S(1)} %get-tuple-element.39), channel_id=1, source_target_pairs={{0,1},{1,0},{2,3},{3,2},{4,5},{5,4},{6,7},{7,6},{8,9},{9,8},{10,11... | collective-permute-start | bytes 110600 | tf_op jit(solution)/shard_map/ppermute | solution.py:733
  12.3 3.6 %collective-permute-start.4 = (f32[24,128]{1,0:T(8,128)S(1)}, f32[24,128]{1,0:T(8,128)S(1)}, u32[]{:S(2)}, u32[]{:S(2)}) collective-permute-start(f32[24,128]{1,0:T(8,128)S(1)} %get-tuple-element.56.refs_1_), channel_id=1, source_target_pairs={{0,1},{1,0},{2,10},{3,11},{4,12},{5,13},{6,14},{7,15},{8,9},{9,8},... | collective-permute-start | bytes 36872 | tf_op jit(solution)/shard_map/ppermute | solution.py:738
  12.4 4.7 %collective-permute-start.5 = (f32[24,128]{1,0:T(8,128)S(1)}, f32[24,128]{1,0:T(8,128)S(1)}, u32[]{:S(2)}, u32[]{:S(2)}) collective-permute-start(f32[24,128]{1,0:T(8,128)S(1)} %get-tuple-element.58), channel_id=1, source_target_pairs={{0,8},{1,2},{2,1},{3,4},{4,3},{5,6},{6,5},{7,15},{8,0},{9,10},{10,... | collective-permute-start | bytes 36872 | tf_op jit(solution)/shard_map/ppermute | solution.py:740
  14.0 3.7 %collective-permute-start.6 = (f32[24,128]{1,0:T(8,128)S(1)}, f32[24,128]{1,0:T(8,128)S(1)}, u32[]{:S(2)}, u32[]{:S(2)}) collective-permute-start(f32[24,128]{1,0:T(8,128)S(1)} %get-tuple-element.59), channel_id=1, source_target_pairs={{0,8},{1,9},{2,3},{3,2},{4,5},{5,4},{6,7},{7,6},{8,0},{9,1},{10,11... | collective-permute-start | bytes 36872 | tf_op jit(solution)/shard_map/ppermute | solution.py:740
where the time goes:
time: 18.6 us; the launch traced here: 18.4 us
  Pallas kernels  7.69 us (41%)
  starting transfers between devices  5.72 us (31%)
  waiting for transfers between devices  4.23 us (23%)
  between operations  0.75 us (4%)
    pallas_call x8, Pallas kernels, call(): pl.pallas_call(kernel, out_shape=out, in_specs=[pl.BlockSpec(memory_space...  7.69 us
    ppermute x1, starting transfers between devices, swap_stream(): far = lax.ppermute(far, 'stream', second)  1.63 us
    ppermute x1, starting transfers between devices, swap_cross_ahead(): lax.ppermute(far, axes, cross_pairs(False))  1.62 us
    ppermute x1, starting transfers between devices, swap_cross(): lax.ppermute(far, axes, cross_pairs(False))  1.61 us
    ppermute x1, waiting for transfers between devices, swap_cross(): lax.ppermute(far, axes, cross_pairs(False))  1.32 us
    ppermute x1, waiting for transfers between devices, swap_cross_ahead(): lax.ppermute(far, axes, cross_pairs(False))  1.1 us
    ppermute x1, waiting for transfers between devices, swap_cross_ahead(): lax.ppermute(near, axes, cross_pairs(True, False))  0.65 us
    ppermute x1, waiting for transfers between devices, swap_cross(): lax.ppermute(near, axes, cross_pairs(True))  0.61 us
  transfers between devices with their start and end apart: 7, of which 5 were waited for; matrix products, arithmetic and copies ran while one was open for 0% of the time, Pallas kernels for 25%

commit v1 on v0

--- a/solution.py
+++ b/solution.py
@@ -513,11 +513,12 @@
         else:
             columns = own_columns_ref[a - 1]
         begin = a * box
-        v_ref[a] = dot(columns, stacked(u[begin : begin + kin]))
         high, low_half = split((spread_rows(first, back_m, face_m) * second_faces)[:, :pairs])
         face_ref[a] = jnp.concatenate([high, low_half], 0)
         total = jnp.sum(pick_p * eigen, 1, keepdims=True) + second_sum
-        rec_ref[a] = 1.0 / (total + e3_row_ref[...])
+        reciprocal = 1.0 / (total + e3_row_ref[...])
+        rec_ref[a] = reciprocal
+        v_ref[a] = dot(columns, stacked(u[begin : begin + kin])) * reciprocal
     blocks = mt_ref.shape[0] // modes
     inner = inner_table(blocks, modes)
     table = sum(
@@ -551,7 +552,7 @@
                 rim += [u[base + start : base + start + 16]]
         rim = jnp.concatenate(rim, 0)
         table = side_rim_ref[min(a, 1)] if a in (0, columns - 1) else own_rim_ref[a - 1]
-        found.append((v_ref[a] + dot(table, stacked(rim))) * rec_ref[a])
+        found.append(v_ref[a] + dot(table, stacked(rim)) * rec_ref[a])
     return found
 
 

time: 18.6 us -> 18.6 us (level)
  no operation moved by 1% of the time
where the time goes in v1:
time: 18.6 us; the launch traced here: 18.4 us
  Pallas kernels  7.75 us (42%)
  starting transfers between devices  5.72 us (31%)
  waiting for transfers between devices  4.16 us (22%)
  between operations  0.75 us (4%)
    pallas_call x8, Pallas kernels, call(): pl.pallas_call(kernel, out_shape=out, in_specs=[pl.BlockSpec(memory_space...  7.75 us
    ppermute x1, starting transfers between devices, swap_stream(): far = lax.ppermute(far, 'stream', second)  1.63 us
    ppermute x1, starting transfers between devices, swap_cross_ahead(): lax.ppermute(far, axes, cross_pairs(False))  1.62 us
    ppermute x1, starting transfers between devices, swap_cross(): lax.ppermute(far, axes, cross_pairs(False))  1.61 us
    ppermute x1, waiting for transfers between devices, swap_cross(): lax.ppermute(far, axes, cross_pairs(False))  1.26 us
    ppermute x1, waiting for transfers between devices, swap_cross_ahead(): lax.ppermute(far, axes, cross_pairs(False))  1.1 us
    ppermute x1, waiting for transfers between devices, swap_cross_ahead(): lax.ppermute(near, axes, cross_pairs(True, False))  0.65 us
    ppermute x1, waiting for transfers between devices, swap_cross(): lax.ppermute(near, axes, cross_pairs(True))  0.61 us
  transfers between devices with their start and end apart: 7, of which 5 were waited for; matrix products, arithmetic and copies ran while one was open for 0% of the time, Pallas kernels for 25%

profile of v1, /device:TPU:18, one launch (start us, length us, event | category | flops | bytes accessed | tf_op | source)
XLA Modules:
  0.0 18.4 jit_solution(16633184709740568038)
XLA Ops:
  0.6 0.0 copy-start
  0.6 1.6 %local_product.1 = (f32[192,128]{1,0:T(8,128)S(1)}, f32[80,128]{1,0:T(8,128)S(1)}, f32[80,128]{1,0:T(8,128)S(1)}, f32[10,3,10]{2,1,0:T(4,128)S(1)}, f32[3,10]{1,0:T(4,128)S(1)}, /*index=5*/f32[1,10]{1,0:T(1,128)S(1)}) custom-call(f32[24,8,128]{2,1,0:T(8,128)} %refs_0_.1, f32[3,24,8,128]{3,2,1,0:T(8,128)} %refs_1_.1, f32[3,24,8,128]{3,2,1,0:T(8,128)} %refs_2_.1, ...), custom_call_target="tpu_custom_call" | custom-call | flops 1000000 | bytes 1000000 | tf_op jit(solution)/shard_map/local_product/pallas_call | solution.py:695
  2.2 0.0 copy-start.1
  2.2 0.1 collective-permute-start
  2.3 0.0 copy-start.2
  2.3 1.6 %collective-permute-start.1 = (f32[80,128]{1,0:T(8,128)S(1)}, f32[80,128]{1,0:T(8,128)S(1)}, u32[]{:S(2)}, u32[]{:S(2)}) collective-permute-start(f32[80,128]{1,0:T(8,128)S(1)} %get-tuple-element.33), channel_id=1, source_target_pairs={{0,24},{8,16},{16,8},{24,0},{1,25},{9,17},{17,9},{25,1},{2,26},{10... | collective-permute-start | bytes 122888 | tf_op jit(solution)/shard_map/ppermute | solution.py:717
  3.9 0.0 copy-done
  3.9 0.0 copy-done.1
  3.9 0.0 copy-done.2
  3.9 1.3 %mode_tables.1 = (bf16[384,160]{1,0:T(8,128)(2,1)S(1)}, f32[1,160]{1,0:T(1,128)S(1)}, bf16[3,112,288]{2,1,0:T(8,128)(2,1)S(1)}, bf16[3,112,192]{2,1,0:T(8,128)(2...) custom-call(f32[160,10]{1,0:T(8,128)S(1)} %bitcast.5, ...), custom_call_target="tpu_custom_call" | custom-call | flops 1000000 | bytes 1000000 | tf_op jit(solution)/shard_map/mode_tables/pallas_call | solution.py:695
  5.3 0.0 collective-permute-done.near_ref.s_near_ref
  5.3 0.5 %collective-permute-done.1.far_ref.s_far_ref = f32[80,128]{1,0:T(8,128)S(1)} collective-permute-done((f32[80,128]{1,0:T(8,128)S(1)}, f32[80,128]{1,0:T(8,128)S(1)}, u32[]{:S(2)}, u32[]{:S(2)}) %collective-permute-start.1) | collective-permute-done | bytes 40992 | tf_op jit(solution)/shard_map/ppermute | solution.py:717
  5.8 0.1 rows_to_send.1
  5.9 1.6 %collective-permute-start.2 = (f32[72,128]{1,0:T(8,128)S(1)}, f32[72,128]{1,0:T(8,128)S(1)}, u32[]{:S(2)}, u32[]{:S(2)}) collective-permute-start(f32[72,128]{1,0:T(8,128)S(1)} %get-tuple-element.38), channel_id=1, source_target_pairs={{0,8},{1,2},{2,1},{3,4},{4,3},{5,6},{6,5},{7,15},{8,0},{9,10},{10,... | collective-permute-start | bytes 110600 | tf_op jit(solution)/shard_map/ppermute | solution.py:734
  7.5 0.4 %collective-permute-start.3 = (f32[72,128]{1,0:T(8,128)S(1)}, f32[72,128]{1,0:T(8,128)S(1)}, u32[]{:S(2)}, u32[]{:S(2)}) collective-permute-start(f32[72,128]{1,0:T(8,128)S(1)} %get-tuple-element.39), channel_id=1, source_target_pairs={{0,1},{1,0},{2,3},{3,2},{4,5},{5,4},{6,7},{7,6},{8,9},{9,8},{10,11... | collective-permute-start | bytes 110600 | tf_op jit(solution)/shard_map/ppermute | solution.py:734
  7.9 1.7 %own_part.1 = (f32[5,112,160]{2,1,0:T(8,128)S(1)}, bf16[2,112,192]{2,1,0:T(8,128)(2,1)S(1)}, f32[5,112,160]{2,1,0:T(8,128)S(1)}, bf16[5,32,112]{2,1,0:T(8,128)(2...) custom-call(f32[192,128]{1,0:T(8,128)S(1)} %get-tuple-element.31.lp_ref, ...), custom_call_target="tpu_custom_call" | custom-call | flops 1000000 | bytes 1000000 | tf_op jit(solution)/shard_map/own_part/pallas_call | solution.py:695
  9.6 1.3 %collective-permute-done.2.far_ref.c_far_ref = f32[72,128]{1,0:T(8,128)S(1)} collective-permute-done((f32[72,128]{1,0:T(8,128)S(1)}, f32[72,128]{1,0:T(8,128)S(1)}, u32[]{:S(2)}, u32[]{:S(2)}) %collective-permute-start.2) | collective-permute-done | bytes 36896 | tf_op jit(solution)/shard_map/ppermute | solution.py:734
  10.9 0.6 %collective-permute-done.3.near_ref.c_near_ref = f32[72,128]{1,0:T(8,128)S(1)} collective-permute-done((f32[72,128]{1,0:T(8,128)S(1)}, f32[72,128]{1,0:T(8,128)S(1)}, u32[]{:S(2)}, u32[]{:S(2)}) %collective-permute-start.3) | collective-permute-done | bytes 36896 | tf_op jit(solution)/shard_map/ppermute | solution.py:734
  11.5 0.8 %faces.1 = (f32[24,128]{1,0:T(8,128)S(1)}, f32[24,128]{1,0:T(8,128)S(1)}, f32[5,112,160]{2,1,0:T(8,128)S(1)}) custom-call(f32[72,128]{1,0:T(8,128)S(1)} %collective-permute-done.2.far_ref.c_far_ref, f32[72,128]{1,0:T(8,128)S(1)} %collective-permute-done.3.near_ref.c_near_ref, bf16[384,160]{1,0:T(8,128)(2,1)S(1)} %get-tuple-element.40.w_ref, ...), custom_call_target="tpu_custom_call" | custom-call | flops 1000000 | bytes 1000000 | tf_op jit(solution)/shard_map/faces/pallas_call | solution.py:695
  12.3 0.1 collective-permute-start.4
  12.4 1.6 %collective-permute-start.5 = (f32[24,128]{1,0:T(8,128)S(1)}, f32[24,128]{1,0:T(8,128)S(1)}, u32[]{:S(2)}, u32[]{:S(2)}) collective-permute-start(f32[24,128]{1,0:T(8,128)S(1)} %get-tuple-element.58), channel_id=1, source_target_pairs={{0,8},{1,2},{2,1},{3,4},{4,3},{5,6},{6,5},{7,15},{8,0},{9,10},{10,... | collective-permute-start | bytes 36872 | tf_op jit(solution)/shard_map/ppermute | solution.py:741
  14.0 0.4 %collective-permute-start.6 = (f32[24,128]{1,0:T(8,128)S(1)}, f32[24,128]{1,0:T(8,128)S(1)}, u32[]{:S(2)}, u32[]{:S(2)}) collective-permute-start(f32[24,128]{1,0:T(8,128)S(1)} %get-tuple-element.59), channel_id=1, source_target_pairs={{0,8},{1,9},{2,3},{3,2},{4,5},{5,4},{6,7},{7,6},{8,0},{9,1},{10,11... | collective-permute-start | bytes 36872 | tf_op jit(solution)/shard_map/ppermute | solution.py:741
  14.4 1.6 %solve.1 = (f32[24,8,128]{2,1,0:T(8,128)}, f32[192,128]{1,0:T(8,128)S(1)}) custom-call(f32[192,128]{1,0:T(8,128)S(1)} %get-tuple-element.31.lp_ref, f32[80,128]{1,0:T(8,128)S(1)} %collective-permute-done.near_ref.s_near_ref, f32[80,128]{1,0:T(8,128)S(1)} %collective-permute-done.1.far_ref.s_far_ref, f32[72,128]{1,0:T(8,128)S(1)} %collective-permute-done.2.far_ref.c_far_ref, ...), custom_call_target="tpu_custom_call" | custom-call | flops 1000000 | bytes 1000000 | tf_op jit(solution)/shard_map/solve/pallas_call | solution.py:695
  16.0 0.0 collective-permute-done.4.ahead_ref
  16.0 1.1 %collective-permute-done.5.far_ref = f32[24,128]{1,0:T(8,128)S(1)} collective-permute-done((f32[24,128]{1,0:T(8,128)S(1)}, f32[24,128]{1,0:T(8,128)S(1)}, u32[]{:S(2)}, u32[]{:S(2)}) %collective-permute-start.5) | collective-permute-done | bytes 12320 | tf_op jit(solution)/shard_map/ppermute | solution.py:741
  17.1 0.7 %collective-permute-done.6.near_ref = f32[24,128]{1,0:T(8,128)S(1)} collective-permute-done((f32[24,128]{1,0:T(8,128)S(1)}, f32[24,128]{1,0:T(8,128)S(1)}, u32[]{:S(2)}, u32[]{:S(2)}) %collective-permute-start.6) | collective-permute-done | bytes 12320 | tf_op jit(solution)/shard_map/ppermute | solution.py:741
  17.7 0.7 %preconditioned.1 = f32[24,8,128]{2,1,0:T(8,128)} custom-call(f32[192,128]{1,0:T(8,128)S(1)} %get-tuple-element.55.r_ref, f32[24,128]{1,0:T(8,128)S(1)} %collective-permute-done.4.ahead_ref, f32[24,128]{1,0:T(8,128)S(1)} %collective-permute-done.5.far_ref, f32[24,128]{1,0:T(8,128)S(1)} %collective-permute-done.6.near_ref), custom_call_target="tpu_custom_call" | custom-call | flops 1000000 | bytes 1000000 | tf_op jit(solution)/shard_map/preconditioned/pallas_call | solution.py:695
  (1 shorter events, 0.0 us)
Async XLA Ops:
  0.6 3.3 %copy-start = (f32[16,10,10]{2,0,1:T(8,128)S(1)}, f32[16,10,10]{2,0,1:T(8,128)}, u32[]{:S(2)}) copy-start(f32[16,10,10]{2,0,1:T(8,128)} %param.14) | copy-start | bytes 19204
  2.2 1.7 %copy-start.1 = (f32[16,10]{1,0:T(8,128)S(1)}, f32[16,10]{1,0:T(8,128)}, u32[]{:S(2)}) copy-start(f32[16,10]{1,0:T(8,128)} %e3_ref.1) | copy-start | bytes 1924
  2.2 3.0 %collective-permute-start = (f32[80,128]{1,0:T(8,128)S(1)}, f32[80,128]{1,0:T(8,128)S(1)}, u32[]{:S(2)}, u32[]{:S(2)}) collective-permute-start(f32[80,128]{1,0:T(8,128)S(1)} %get-tuple-element.32), channel_id=1, source_target_pairs={{0,8},{8,0},{16,24},{24,16},{1,9},{9,1},{17,25},{25,17},{2,10},{10... | collective-permute-start | bytes 122888 | tf_op jit(solution)/shard_map/ppermute | solution.py:716
  2.3 1.6 %copy-start.2 = (f32[1,10,10]{2,0,1:T(1,128)S(1)}, f32[1,10,10]{2,0,1:T(1,128)}, u32[]{:S(2)}) copy-start(f32[1,10,10]{2,0,1:T(1,128)} %param.13) | copy-start | bytes 1204
  2.3 3.5 %collective-permute-start.1 = (f32[80,128]{1,0:T(8,128)S(1)}, f32[80,128]{1,0:T(8,128)S(1)}, u32[]{:S(2)}, u32[]{:S(2)}) collective-permute-start(f32[80,128]{1,0:T(8,128)S(1)} %get-tuple-element.33), channel_id=1, source_target_pairs={{0,24},{8,16},{16,8},{24,0},{1,25},{9,17},{17,9},{25,1},{2,26},{10... | collective-permute-start | bytes 122888 | tf_op jit(solution)/shard_map/ppermute | solution.py:717
  5.9 5.0 %collective-permute-start.2 = (f32[72,128]{1,0:T(8,128)S(1)}, f32[72,128]{1,0:T(8,128)S(1)}, u32[]{:S(2)}, u32[]{:S(2)}) collective-permute-start(f32[72,128]{1,0:T(8,128)S(1)} %get-tuple-element.38), channel_id=1, source_target_pairs={{0,8},{1,2},{2,1},{3,4},{4,3},{5,6},{6,5},{7,15},{8,0},{9,10},{10,... | collective-permute-start | bytes 110600 | tf_op jit(solution)/shard_map/ppermute | solution.py:734
  7.5 4.0 %collective-permute-start.3 = (f32[72,128]{1,0:T(8,128)S(1)}, f32[72,128]{1,0:T(8,128)S(1)}, u32[]{:S(2)}, u32[]{:S(2)}) collective-permute-start(f32[72,128]{1,0:T(8,128)S(1)} %get-tuple-element.39), channel_id=1, source_target_pairs={{0,1},{1,0},{2,3},{3,2},{4,5},{5,4},{6,7},{7,6},{8,9},{9,8},{10,11... | collective-permute-start | bytes 110600 | tf_op jit(solution)/shard_map/ppermute | solution.py:734
  12.3 3.6 %collective-permute-start.4 = (f32[24,128]{1,0:T(8,128)S(1)}, f32[24,128]{1,0:T(8,128)S(1)}, u32[]{:S(2)}, u32[]{:S(2)}) collective-permute-start(f32[24,128]{1,0:T(8,128)S(1)} %get-tuple-element.56.refs_1_), channel_id=1, source_target_pairs={{0,1},{1,0},{2,10},{3,11},{4,12},{5,13},{6,14},{7,15},{8,9},{9,8},... | collective-permute-start | bytes 36872 | tf_op jit(solution)/shard_map/ppermute | solution.py:739
  12.4 4.7 %collective-permute-start.5 = (f32[24,128]{1,0:T(8,128)S(1)}, f32[24,128]{1,0:T(8,128)S(1)}, u32[]{:S(2)}, u32[]{:S(2)}) collective-permute-start(f32[24,128]{1,0:T(8,128)S(1)} %get-tuple-element.58), channel_id=1, source_target_pairs={{0,8},{1,2},{2,1},{3,4},{4,3},{5,6},{6,5},{7,15},{8,0},{9,10},{10,... | collective-permute-start | bytes 36872 | tf_op jit(solution)/shard_map/ppermute | solution.py:741
  14.0 3.7 %collective-permute-start.6 = (f32[24,128]{1,0:T(8,128)S(1)}, f32[24,128]{1,0:T(8,128)S(1)}, u32[]{:S(2)}, u32[]{:S(2)}) collective-permute-start(f32[24,128]{1,0:T(8,128)S(1)} %get-tuple-element.59), channel_id=1, source_target_pairs={{0,8},{1,9},{2,3},{3,2},{4,5},{5,4},{6,7},{7,6},{8,0},{9,1},{10,11... | collective-permute-start | bytes 36872 | tf_op jit(solution)/shard_map/ppermute | solution.py:741
